TPU v7x, 32 devices: a whole 2x2x4 slice. The times are simulated.
32 devices in a mesh: segment: 4 (over x, core), tensor: 8 (over z, y).
Axes of the slice: x: 2, y: 2, z: 4, core: 2. Of those that a mesh axis runs over, the one named last changes fastest.
Arguments:
- embeds: bfloat16 [2, 16, 6144], P(None, None, 'tensor'), may hold values from -6 to 6
- norm_gains: float32 [4, 2, 6144], P('segment'), may hold values from 0.5 to 2
- w_qkv: bfloat16 [4, 6144, 3, 8, 128], P('segment', None, None, 'tensor'), may hold values from -0.078125 to 0.078125
- w_out: bfloat16 [4, 8, 128, 6144], P('segment', 'tensor'), may hold values from -0.1875 to 0.1875
- w_up: bfloat16 [4, 6144, 1024], P('segment', None, 'tensor'), may hold values from -0.078125 to 0.078125
- w_down: bfloat16 [4, 1024, 6144], P('segment', 'tensor'), may hold values from -0.1875 to 0.1875
- cache: bfloat16 [4, 2, 16, 8, 64, 128], P('segment', None, None, 'tensor')
- lengths: int32 [16], replicated, may hold values from 1 to 64, as said below
- active_heads: int32 [4, 2, 2, 8], P('segment'), may hold values from 0 to 7, as said below
- active_blocks: int32 [4, 2, 2, 8], P('segment'), may hold values from 0 to 7, as said below
- active_counts: int32 [4, 2, 2, 2], P('segment'), may hold values from 1 to 8, as said below
Outputs:
- states: bfloat16 [4, 2, 16, 6144], P('segment', None, None, 'tensor')
Inputs may be any that keep to these rules, and one draw needn't show every extreme that they name: `active_heads`: the first active_counts[...,0] entries of a list are distinct heads, the rest are 0. `active_blocks`: the first active_counts[...,1] entries of a list are distinct blocks, the rest are 0. `active_counts`: every list is full for the first micro-batch of the first step. `lengths`: some sequence has all 64 positions live.
All inputs are finite; a program needn't handle non-finite values.
Results may differ from a plain program's by a relative error of at most 0.024.
Values may be sent and summed in bfloat16 or wider, within the bound.
A program may use at most 64 MiB of HBM per device.

v0:
```python
import jax
import jax.numpy as jnp
from jax import lax
from jax.sharding import PartitionSpec as P

EPS = 1e-05


def shifted(array, axis, by):
    length = lax.axis_size(axis)
    pairs = [(i, i + by) for i in range(length) if 0 <= i + by < length]
    return lax.ppermute(array, axis, pairs)


def normalize_whole(x, gain):
    values = x.astype(jnp.float32)
    mean = jnp.mean(values, -1, keepdims=True)
    var = jnp.mean((values - mean) ** 2, -1, keepdims=True)
    return ((values - mean) * lax.rsqrt(var + EPS) * gain).astype(jnp.bfloat16)


def body(
    embeds,
    norm_gains,
    w_qkv,
    w_out,
    w_up,
    w_down,
    cache,
    lengths,
    active_heads,
    active_blocks,
    active_counts,
):
    segments = lax.axis_size("segment")
    segment = lax.axis_index("segment")
    rank = lax.axis_index("tensor")
    members = lax.axis_size("tensor")
    steps_n, seqs, piece = embeds.shape
    width = piece * members
    micro = active_heads.shape[2]
    group = seqs // micro
    head_dim = w_qkv.shape[-1]
    positions = cache.shape[4]
    items = steps_n * micro
    ticks = segments + items - 1
    scale = head_dim ** (-0.5)
    head_slots = jnp.arange(active_heads.shape[-1]) < active_counts[0, :, :, 0, None]
    head_live = jnp.any((active_heads[0] == rank) & head_slots, -1)
    block_slots = jnp.arange(active_blocks.shape[-1]) < active_counts[0, :, :, 1, None]
    block_live = jnp.any((active_blocks[0] == rank) & block_slots, -1)
    projection = w_qkv.reshape(width, 3 * head_dim)
    out_proj = w_out[0, 0]
    up_w = w_up[0]
    down_w = w_down[0]
    keys_all = cache[0, 0, :, 0]
    values_all = cache[0, 1, :, 0]
    gain_attn = norm_gains[0, 0]
    gain_feed = norm_gains[0, 1]

    def normalize(x, gain):
        return normalize_whole(x, gain)

    def attend(h, fresh, step, batch):
        qkv = (
            jnp.dot(h, projection, preferred_element_type=jnp.float32)
            .astype(jnp.bfloat16)
            .reshape(group, 3, head_dim)
        )
        start = batch * group
        stacked = jnp.stack([qkv[:, 1], qkv[:, 2]])[None]
        fresh = lax.dynamic_update_slice(fresh, stacked, (step, 0, start, 0))

        def look(query):
            keys = lax.dynamic_slice_in_dim(keys_all, start, group, 0)
            values = lax.dynamic_slice_in_dim(values_all, start, group, 0)
            live = (
                jnp.arange(positions)[None, :]
                < lax.dynamic_slice_in_dim(lengths, start, group)[:, None]
            )
            old = jnp.einsum("sk,spk->sp", query, keys, preferred_element_type=jnp.float32) * scale
            old = jnp.where(live, old, -jnp.inf)
            mine = lax.dynamic_slice_in_dim(fresh, start, group, 2)
            new = (
                jnp.einsum("sk,usk->su", query, mine[:, 0], preferred_element_type=jnp.float32)
                * scale
            )
            new = jnp.where(jnp.arange(steps_n)[None, :] <= step, new, -jnp.inf)
            probs = jax.nn.softmax(jnp.concatenate([old, new], -1), -1).astype(jnp.bfloat16)
            mixed = jnp.einsum(
                "sp,spk->sk", probs[:, :positions], values, preferred_element_type=jnp.float32
            )
            mixed = mixed + jnp.einsum(
                "su,usk->sk", probs[:, positions:], mine[:, 1], preferred_element_type=jnp.float32
            )
            return jnp.dot(mixed.astype(jnp.bfloat16), out_proj, preferred_element_type=jnp.float32)

        def silent(query):
            return jnp.zeros((group, width), jnp.float32)

        partial_value = lax.cond(head_live[step, batch], look, silent, qkv[:, 0])
        return (partial_value, fresh)

    def feed(h2):
        active = jax.nn.relu(jnp.dot(h2, up_w, preferred_element_type=jnp.float32)).astype(
            jnp.bfloat16
        )
        return jnp.dot(active, down_w, preferred_element_type=jnp.float32)

    def quiet(h2):
        return jnp.zeros((group, width), jnp.float32)

    def layer(x, fresh, step, batch):
        h = normalize(x, gain_attn)
        partial_value, fresh = attend(h, fresh, step, batch)
        first = (x.astype(jnp.float32) + lax.psum(partial_value, "tensor")).astype(jnp.bfloat16)
        second_in = normalize(first, gain_feed)
        lower = lax.cond(block_live[step, batch], feed, quiet, second_in)
        result = (first.astype(jnp.float32) + lax.psum(lower, "tensor")).astype(jnp.bfloat16)
        return (result, fresh)

    source = lax.all_gather(embeds, "tensor", axis=2, tiled=True)
    columns = source.shape[2]

    def tick(index, carry):
        received, fresh, states = carry
        item = index - segment
        valid = (item >= 0) & (item < items)
        safe = jnp.clip(item, 0, items - 1)
        step = safe // micro
        batch = safe % micro
        fed = lax.dynamic_slice(source, (step, batch * group, 0), (1, group, columns))[0]
        x = jnp.where(segment == 0, fed, received)
        computed, fresh_new = layer(x, fresh, step, batch)
        fresh = jnp.where(valid, fresh_new, fresh)
        result = jnp.where(valid, computed, x)
        kept = lax.dynamic_slice_in_dim(result, rank * piece, piece, 1)
        previous = lax.dynamic_slice(states, (step, batch * group, 0), (1, group, piece))[0]
        states = lax.dynamic_update_slice(
            states, jnp.where(valid, kept, previous)[None], (step, batch * group, 0)
        )
        sent = shifted(result, "segment", 1)
        return (sent, fresh, states)

    start_state = jnp.zeros((group, columns), jnp.bfloat16)
    start_fresh = jnp.zeros((steps_n, 2, seqs, head_dim), jnp.bfloat16)
    start_out = jnp.zeros((steps_n, seqs, piece), jnp.bfloat16)
    final = lax.fori_loop(0, ticks, tick, (start_state, start_fresh, start_out))
    return final[2][None]


def solution(mesh):
    in_specs = (
        P(None, None, "tensor"),
        P("segment", None, None),
        P("segment", None, None, "tensor", None),
        P("segment", "tensor", None, None),
        P("segment", None, "tensor"),
        P("segment", "tensor", None),
        P("segment", None, None, "tensor", None, None),
        P(),
        P("segment", None, None, None),
        P("segment", None, None, None),
        P("segment", None, None, None),
    )
    out_specs = P("segment", None, None, "tensor")
    return jax.shard_map(body, mesh=mesh, in_specs=in_specs, out_specs=out_specs, check_vma=False)
```

profile of v0, /device:TPU:3, one launch (start us, length us, event | category | flops | bytes accessed | tf_op | source)
XLA Modules:
  0.0 1205.9 jit_solution(16473897109475222066)
XLA Ops:
  12.3 6.7 copy.21
  19.0 6.8 copy.24
  25.8 27.0 %all_gather.3 = bf16[2,16,6144]{2,1,0:T(8,128)(2,1)} all-gather(bf16[2,16,768]{2,1,0:T(8,128)(2,1)S(1)} %copy-done.4), channel_id=1, replica_groups=mesh['segment'=4,'tensor'=8] {'tensor'}, dimensions={2}, use_global_device_ids=true | all-gather | bytes 442368 | tf_op jit(solution)/shard_map/all_gather | solution.py:122
  53.5 1145.9 %while.20 = (s32[]{:T(128)}, bf16[8,6144]{1,0:T(8,128)(2,1)S(1)}, bf16[2,2,16,128]{3,2,1,0:T(8,128)(2,1)}, bf16[2,16,768]{2,1,0:T(8,128)(2,1)}, s32[]{:T(128)}, ...) while((s32[]{:T(128)}, bf16[8,6144]{1,0:T(8,128)(2,1)S(1)}, ...), condition=%wide.region_16.17_spmd.clone, body=%wide.region_2.16_spmd.clone.sunk | while | flops 77392576 | bytes 16468786 | solution.py:148
  59.9 4.2 conditional.6
  68.1 72.3 %all-reduce.3.cloned.1.call-done = f32[8,6144]{1,0:T(8,128)} async-done(((f32[8,6144]{1,0:T(8,128)}), f32[8,6144]{1,0:T(8,128)}) %all-reduce.3.cloned.1.call-update) | async-done | bytes 196624 | tf_op jit(solution)/shard_map/while/body/eval_jaxpr/psum | solution.py:116
  146.6 68.6 %all-reduce.5.cloned.1.call-done = f32[8,6144]{1,0:T(8,128)} async-done(((f32[8,6144]{1,0:T(8,128)}), f32[8,6144]{1,0:T(8,128)}) %all-reduce.5.cloned.1.call-update) | async-done | bytes 196624 | tf_op jit(solution)/shard_map/while/body/eval_jaxpr/psum | solution.py:119
  228.6 4.1 conditional.6
  236.8 66.6 %all-reduce.3.cloned.1.call-done = f32[8,6144]{1,0:T(8,128)} async-done(((f32[8,6144]{1,0:T(8,128)}), f32[8,6144]{1,0:T(8,128)}) %all-reduce.3.cloned.1.call-update) | async-done | bytes 196624 | tf_op jit(solution)/shard_map/while/body/eval_jaxpr/psum | solution.py:116
  310.3 67.9 %all-reduce.5.cloned.1.call-done = f32[8,6144]{1,0:T(8,128)} async-done(((f32[8,6144]{1,0:T(8,128)}), f32[8,6144]{1,0:T(8,128)}) %all-reduce.5.cloned.1.call-update) | async-done | bytes 196624 | tf_op jit(solution)/shard_map/while/body/eval_jaxpr/psum | solution.py:119
  391.6 4.1 conditional.6
  399.7 66.6 %all-reduce.3.cloned.1.call-done = f32[8,6144]{1,0:T(8,128)} async-done(((f32[8,6144]{1,0:T(8,128)}), f32[8,6144]{1,0:T(8,128)}) %all-reduce.3.cloned.1.call-update) | async-done | bytes 196624 | tf_op jit(solution)/shard_map/while/body/eval_jaxpr/psum | solution.py:116
  473.3 67.9 %all-reduce.5.cloned.1.call-done = f32[8,6144]{1,0:T(8,128)} async-done(((f32[8,6144]{1,0:T(8,128)}), f32[8,6144]{1,0:T(8,128)}) %all-reduce.5.cloned.1.call-update) | async-done | bytes 196624 | tf_op jit(solution)/shard_map/while/body/eval_jaxpr/psum | solution.py:119
  554.6 4.1 conditional.6
  562.7 66.6 %all-reduce.3.cloned.1.call-done = f32[8,6144]{1,0:T(8,128)} async-done(((f32[8,6144]{1,0:T(8,128)}), f32[8,6144]{1,0:T(8,128)}) %all-reduce.3.cloned.1.call-update) | async-done | bytes 196624 | tf_op jit(solution)/shard_map/while/body/eval_jaxpr/psum | solution.py:116
  636.3 67.9 %all-reduce.5.cloned.1.call-done = f32[8,6144]{1,0:T(8,128)} async-done(((f32[8,6144]{1,0:T(8,128)}), f32[8,6144]{1,0:T(8,128)}) %all-reduce.5.cloned.1.call-update) | async-done | bytes 196624 | tf_op jit(solution)/shard_map/while/body/eval_jaxpr/psum | solution.py:119
  717.6 4.1 conditional.6
  725.8 66.6 %all-reduce.3.cloned.1.call-done = f32[8,6144]{1,0:T(8,128)} async-done(((f32[8,6144]{1,0:T(8,128)}), f32[8,6144]{1,0:T(8,128)}) %all-reduce.3.cloned.1.call-update) | async-done | bytes 196624 | tf_op jit(solution)/shard_map/while/body/eval_jaxpr/psum | solution.py:116
  799.3 68.0 %all-reduce.5.cloned.1.call-done = f32[8,6144]{1,0:T(8,128)} async-done(((f32[8,6144]{1,0:T(8,128)}), f32[8,6144]{1,0:T(8,128)}) %all-reduce.5.cloned.1.call-update) | async-done | bytes 196624 | tf_op jit(solution)/shard_map/while/body/eval_jaxpr/psum | solution.py:119
  880.6 4.1 conditional.6
  888.8 66.6 %all-reduce.3.cloned.1.call-done = f32[8,6144]{1,0:T(8,128)} async-done(((f32[8,6144]{1,0:T(8,128)}), f32[8,6144]{1,0:T(8,128)}) %all-reduce.3.cloned.1.call-update) | async-done | bytes 196624 | tf_op jit(solution)/shard_map/while/body/eval_jaxpr/psum | solution.py:116
  962.3 67.9 %all-reduce.5.cloned.1.call-done = f32[8,6144]{1,0:T(8,128)} async-done(((f32[8,6144]{1,0:T(8,128)}), f32[8,6144]{1,0:T(8,128)}) %all-reduce.5.cloned.1.call-update) | async-done | bytes 196624 | tf_op jit(solution)/shard_map/while/body/eval_jaxpr/psum | solution.py:119
  1051.8 66.6 %all-reduce.3.cloned.1.call-done = f32[8,6144]{1,0:T(8,128)} async-done(((f32[8,6144]{1,0:T(8,128)}), f32[8,6144]{1,0:T(8,128)}) %all-reduce.3.cloned.1.call-update) | async-done | bytes 196624 | tf_op jit(solution)/shard_map/while/body/eval_jaxpr/psum | solution.py:116
  1123.2 70.0 %all-reduce.5.cloned.1.call-done = f32[8,6144]{1,0:T(8,128)} async-done(((f32[8,6144]{1,0:T(8,128)}), f32[8,6144]{1,0:T(8,128)}) %all-reduce.5.cloned.1.call-update) | async-done | bytes 196624 | tf_op jit(solution)/shard_map/while/body/eval_jaxpr/psum | solution.py:119
  (343 shorter events, 208.6 us)
Async XLA Ops:
  19.0 6.8 copy-start.4
  19.0 34.4 %copy-start = (bf16[1,1,128,6144]{3,2,1,0:T(8,128)(2,1)S(1)}, bf16[1,1,128,6144]{3,2,1,0:T(8,128)(2,1)}, u32[]{:S(2)}) copy-start(bf16[1,1,128,6144]{3,2,1,0:T(8,128)(2,1)} %param.20) | copy-start | bytes 4718596
  19.0 34.4 %copy-start.1 = (bf16[1,6144,128]{2,1,0:T(8,128)(2,1)S(1)}, bf16[1,6144,128]{2,1,0:T(8,128)(2,1)}, u32[]{:S(2)}) copy-start(bf16[1,6144,128]{2,1,0:T(8,128)(2,1)} %param.21) | copy-start | bytes 4718596
  53.5 87.0 %all-reduce.3.cloned.1.call-start = ((), (), s32[]{:S(2)}) async-start(), calls=%async_computation | async-start | bytes 393216 | tf_op jit(solution)/shard_map/while/body/eval_jaxpr/psum | solution.py:116
  64.8 150.4 %all-reduce.5.cloned.1.call-start = ((), (), s32[]{:S(2)}) async-start(), calls=%async_computation.1 | async-start | bytes 393216 | tf_op jit(solution)/shard_map/while/body/eval_jaxpr/psum | solution.py:119
  216.2 5.3 collective-permute-start
  221.5 81.9 %all-reduce.3.cloned.1.call-start = ((), (), s32[]{:S(2)}) async-start(), calls=%async_computation | async-start | bytes 393216 | tf_op jit(solution)/shard_map/while/body/eval_jaxpr/psum | solution.py:116
  233.4 144.8 %all-reduce.5.cloned.1.call-start = ((), (), s32[]{:S(2)}) async-start(), calls=%async_computation.1 | async-start | bytes 393216 | tf_op jit(solution)/shard_map/while/body/eval_jaxpr/psum | solution.py:119
  379.2 5.3 collective-permute-start
  384.4 81.9 %all-reduce.3.cloned.1.call-start = ((), (), s32[]{:S(2)}) async-start(), calls=%async_computation | async-start | bytes 393216 | tf_op jit(solution)/shard_map/while/body/eval_jaxpr/psum | solution.py:116
  396.4 144.8 %all-reduce.5.cloned.1.call-start = ((), (), s32[]{:S(2)}) async-start(), calls=%async_computation.1 | async-start | bytes 393216 | tf_op jit(solution)/shard_map/while/body/eval_jaxpr/psum | solution.py:119
  542.2 5.3 collective-permute-start
  547.4 81.9 %all-reduce.3.cloned.1.call-start = ((), (), s32[]{:S(2)}) async-start(), calls=%async_computation | async-start | bytes 393216 | tf_op jit(solution)/shard_map/while/body/eval_jaxpr/psum | solution.py:116
  559.4 144.8 %all-reduce.5.cloned.1.call-start = ((), (), s32[]{:S(2)}) async-start(), calls=%async_computation.1 | async-start | bytes 393216 | tf_op jit(solution)/shard_map/while/body/eval_jaxpr/psum | solution.py:119
  705.2 5.3 collective-permute-start
  710.5 81.9 %all-reduce.3.cloned.1.call-start = ((), (), s32[]{:S(2)}) async-start(), calls=%async_computation | async-start | bytes 393216 | tf_op jit(solution)/shard_map/while/body/eval_jaxpr/psum | solution.py:116
  722.4 144.8 %all-reduce.5.cloned.1.call-start = ((), (), s32[]{:S(2)}) async-start(), calls=%async_computation.1 | async-start | bytes 393216 | tf_op jit(solution)/shard_map/while/body/eval_jaxpr/psum | solution.py:119
  868.2 5.3 collective-permute-start
  873.5 81.9 %all-reduce.3.cloned.1.call-start = ((), (), s32[]{:S(2)}) async-start(), calls=%async_computation | async-start | bytes 393216 | tf_op jit(solution)/shard_map/while/body/eval_jaxpr/psum | solution.py:116
  885.5 144.8 %all-reduce.5.cloned.1.call-start = ((), (), s32[]{:S(2)}) async-start(), calls=%async_computation.1 | async-start | bytes 393216 | tf_op jit(solution)/shard_map/while/body/eval_jaxpr/psum | solution.py:119
  1031.2 5.3 collective-permute-start
  1036.4 81.9 %all-reduce.3.cloned.1.call-start = ((), (), s32[]{:S(2)}) async-start(), calls=%async_computation | async-start | bytes 393216 | tf_op jit(solution)/shard_map/while/body/eval_jaxpr/psum | solution.py:116
  1048.4 144.7 %all-reduce.5.cloned.1.call-start = ((), (), s32[]{:S(2)}) async-start(), calls=%async_computation.1 | async-start | bytes 393216 | tf_op jit(solution)/shard_map/while/body/eval_jaxpr/psum | solution.py:119
  1194.1 5.3 collective-permute-start
  (14 other events, 9.5 us)
Sparse Core Ops, SparseCore 0:
  64.9 75.4 all-reduce.2
  146.1 69.0 all-reduce.4
  233.6 69.7 all-reduce.2
  309.1 69.0 all-reduce.4
  396.5 69.7 all-reduce.2
  472.1 69.0 all-reduce.4
  559.5 69.7 all-reduce.2
  635.1 69.0 all-reduce.4
  722.6 69.7 all-reduce.2
  798.1 69.1 all-reduce.4
  885.6 69.7 all-reduce.2
  961.1 69.0 all-reduce.4
  1048.6 69.7 all-reduce.2
  1122.0 71.1 all-reduce.4
where the time goes:
time: 1210 us
  waiting for transfers between devices  969 us (80%)
  other arithmetic  63.4 us (5%)
  local copies, waits for them, and re-layouts  61 us (5%)
  matrix products  53.1 us (4%)
  blocking collectives  27 us (2%)
  between operations  13.1 us (1%)
    psum x7, waiting for transfers between devices, layer(): lax.psum(lower, 'tensor')  478 us
    psum x7, waiting for transfers between devices, layer(): lax.psum(partial_value, 'tensor')  472 us
    all_gather x1, blocking collectives, body(): source = lax.all_gather(embeds, 'tensor', axis=2, tiled=True)  27 us
  transfers between devices with their start and end apart: 21, of which 21 were waited for; matrix products, arithmetic and copies ran while one was open for 3% of the time, Pallas kernels for 0%

commit v1 on v0

v1 whole, which is shorter than its diff:
```python
import functools

import jax
import jax.numpy as jnp
from jax import lax
from jax.experimental import pallas as pl
from jax.experimental.pallas import tpu as pltpu
from jax.sharding import PartitionSpec as P

EPS = 1e-05
GROUPS = 1
MESH_ID = pl.DeviceIdType.MESH


def partner_order(members):
    return sorted(range(1, members), key=lambda k: (-min(k, members - k), k))


def relay_kernel(
    sizes,
    embeds,
    gains,
    w_qkv,
    w_out,
    w_up,
    w_down,
    cache,
    lengths,
    heads,
    blocks,
    counts,
    out,
    qkv_w,
    out_w,
    up_w,
    down_w,
    kv,
    load_sem,
    x_in,
    first_in,
    part_out,
    part_in,
    x_recv,
    first_recv,
    part_recv,
    x_send,
    first_send,
    part_send,
    next_send,
    first_own,
    next_own,
):
    segments, members, steps, seqs, micro, groups = sizes
    piece = embeds.shape[1]
    width = piece * members
    rows = steps * seqs // groups
    steps_in = steps // groups
    head_dim = w_qkv.shape[2]
    positions = cache.shape[1] // seqs
    group = seqs // micro
    segment = lax.axis_index("segment")
    rank = lax.axis_index("tensor")
    order = partner_order(members)

    def other(k):
        return lax.rem(rank + k, members)

    loads = [
        pltpu.make_async_copy(
            w_qkv.at[j], qkv_w.at[:, pl.ds(j * head_dim, head_dim)], load_sem.at[j]
        )
        for j in range(3)
    ]
    loads.append(pltpu.make_async_copy(cache, kv, load_sem.at[3]))
    loads.append(pltpu.make_async_copy(w_out, out_w, load_sem.at[4]))
    loads.append(pltpu.make_async_copy(w_up, up_w, load_sem.at[5]))
    loads.append(pltpu.make_async_copy(w_down, down_w, load_sem.at[6]))
    for load in loads:
        load.start()

    barrier = pltpu.get_barrier_semaphore()
    for k in range(1, members):
        pl.semaphore_signal(barrier, inc=1, device_id=(segment, other(k)), device_id_type=MESH_ID)

    @pl.when(segment > 0)
    def _():
        for k in range(members):
            pl.semaphore_signal(
                barrier, inc=1, device_id=(segment - 1, other(k)), device_id_type=MESH_ID
            )

    @pl.when(segment < segments - 1)
    def _():
        for k in range(members):
            pl.semaphore_signal(
                barrier, inc=1, device_id=(segment + 1, other(k)), device_id_type=MESH_ID
            )

    inner = (segment > 0) & (segment < segments - 1)

    @pl.when(inner)
    def _():
        pl.semaphore_wait(barrier, 3 * members - 1)

    @pl.when(jnp.logical_not(inner))
    def _():
        pl.semaphore_wait(barrier, 2 * members - 1)

    def send(src, dst, send_sem, recv_sem, target):
        return pltpu.make_async_remote_copy(
            src_ref=src,
            dst_ref=dst,
            send_sem=send_sem,
            recv_sem=recv_sem,
            device_id=target,
            device_id_type=MESH_ID,
        )

    def arrival(buffer, sem):
        return send(buffer, buffer, sem, sem, (segment, other(1)))

    def x_copy(g, k):
        return send(
            embeds.at[pl.ds(g * rows, rows)],
            x_in.at[g, rank],
            x_send.at[g, k],
            x_recv.at[g, rank],
            (segment, other(k)),
        )

    @pl.when(segment == 0)
    def _():
        for g in range(groups):
            for k in order:
                x_copy(g, k).start()
            x_in[g, rank] = embeds[g * rows : (g + 1) * rows]

    row_ids = lax.broadcasted_iota(jnp.int32, (steps * seqs, 1), 0)
    row_seq = lax.rem(row_ids, seqs)
    row_len = jnp.zeros((steps * seqs, 1), jnp.int32)
    for s in range(seqs):
        row_len = jnp.where(row_seq == s, lengths[s], row_len)

    def live_rows(lists, which):
        live = jnp.zeros((steps * seqs, 1), jnp.int32)
        for t in range(steps):
            for m in range(micro):
                hit = jnp.int32(0)
                for j in range(lists.shape[2]):
                    same = (lists[t, m, j] == rank) & (j < counts[t, m, which])
                    hit = hit + same.astype(jnp.int32)
                start = t * seqs + m * group
                inside = (row_ids >= start) & (row_ids < start + group)
                live = jnp.where(inside, hit, live)
        return live > 0

    head_live = live_rows(heads, 0)
    block_live = live_rows(blocks, 1)

    def span(p):
        return slice(p * piece, (p + 1) * piece)

    def normalized(buffer, g, which):
        total = jnp.zeros((rows, 1), jnp.float32)
        for p in range(members):
            total = total + jnp.sum(buffer[g, p].astype(jnp.float32), -1, keepdims=True)
        mean = total / width
        square = jnp.zeros((rows, 1), jnp.float32)
        for p in range(members):
            off = buffer[g, p].astype(jnp.float32) - mean
            square = square + jnp.sum(off * off, -1, keepdims=True)
        inverse = lax.rsqrt(square / width + EPS)
        for p in range(members):
            off = buffer[g, p].astype(jnp.float32) - mean
            yield p, (off * inverse * gains[which : which + 1, span(p)]).astype(jnp.bfloat16)

    def columns(p):
        return pl.ds(pl.multiple_of(p * piece, piece), piece)

    def part_copy(phase, g, k):
        return send(
            part_out.at[phase, g, k],
            part_in.at[phase, g, rank],
            part_send.at[phase, g, k],
            part_recv.at[phase, g, rank],
            (segment, other(k)),
        )

    def scatter(values, weight, phase, g):
        for k in order:
            part = jnp.dot(values, weight[:, columns(other(k))], preferred_element_type=jnp.float32)
            part_out[phase, g, k] = part.astype(jnp.bfloat16)
            part_copy(phase, g, k).start()
        return jnp.dot(values, weight[:, columns(rank)], preferred_element_type=jnp.float32)

    def gather_sum(total, phase, g):
        for k in reversed(order):
            p = other(k)
            arrival(part_in.at[phase, g, p], part_recv.at[phase, g, p]).wait_recv()
            total = total + part_in[phase, g, p].astype(jnp.float32)
        return total

    def first_copy(g, k):
        return send(
            first_own.at[g],
            first_in.at[g, rank],
            first_send.at[g, k],
            first_recv.at[g, rank],
            (segment, other(k)),
        )

    def next_copy(g, k):
        return send(
            next_own.at[g],
            x_in.at[g, rank],
            next_send.at[g, k],
            x_recv.at[g, rank],
            (segment + 1, other(k)),
        )

    fresh_keys, fresh_values = [], []

    def attend(g):
        qkv = jnp.zeros((rows, 3 * head_dim), jnp.float32)
        for p, h in normalized(x_in, g, 0):
            qkv = qkv + jnp.dot(h, qkv_w[span(p), :], preferred_element_type=jnp.float32)
        qkv = qkv.astype(jnp.bfloat16)
        query = qkv[:, :head_dim]
        fresh_keys.append(qkv[:, head_dim : 2 * head_dim])
        fresh_values.append(qkv[:, 2 * head_dim :])
        scale = head_dim ** (-0.5)
        contract = (((1,), (1,)), ((), ()))
        mine = slice(g * rows, (g + 1) * rows)
        old = lax.dot_general(query, kv[0], contract, preferred_element_type=jnp.float32) * scale
        where = lax.broadcasted_iota(jnp.int32, old.shape, 1)
        start = row_seq[mine] * positions
        live = (where >= start) & (where < start + row_len[mine])
        old = jnp.where(live, old, -jnp.inf)
        top = jnp.max(old, -1, keepdims=True)
        fresh = []
        for u, keys in enumerate(fresh_keys):
            new = lax.dot_general(query, keys, contract, preferred_element_type=jnp.float32) * scale
            seen = lax.broadcasted_iota(jnp.int32, new.shape, 1) + u * rows
            seen_ok = (lax.rem(seen, seqs) == row_seq[mine]) & (seen <= row_ids[mine])
            new = jnp.where(seen_ok, new, -jnp.inf)
            top = jnp.maximum(top, jnp.max(new, -1, keepdims=True))
            fresh.append(new)
        old = jnp.exp(old - top)
        norm = jnp.sum(old, -1, keepdims=True)
        fresh = [jnp.exp(new - top) for new in fresh]
        for new in fresh:
            norm = norm + jnp.sum(new, -1, keepdims=True)
        mixed = jnp.dot(
            (old / norm).astype(jnp.bfloat16), kv[1], preferred_element_type=jnp.float32
        )
        for new, values in zip(fresh, fresh_values):
            mixed = mixed + jnp.dot(
                (new / norm).astype(jnp.bfloat16), values, preferred_element_type=jnp.float32
            )
        return jnp.where(head_live[mine], mixed, 0.0).astype(jnp.bfloat16)

    def feed(g):
        upper = jnp.zeros((rows, up_w.shape[1]), jnp.float32)
        for p, h in normalized(first_in, g, 1):
            upper = upper + jnp.dot(h, up_w[span(p), :], preferred_element_type=jnp.float32)
        mine = slice(g * rows, (g + 1) * rows)
        return jnp.where(block_live[mine], jnp.maximum(upper, 0.0), 0.0).astype(jnp.bfloat16)

    sums = [None] * groups
    for g in range(groups):
        for k in order:
            p = other(k)
            arrival(x_in.at[g, p], x_recv.at[g, p]).wait_recv()

        @pl.when(segment > 0)
        def _():
            arrival(x_in.at[g, rank], x_recv.at[g, rank]).wait_recv()

        if g == 0:
            for load in loads[:4]:
                load.wait()
        mixed = attend(g)
        if g == 0:
            loads[4].wait()
        sums[g] = scatter(mixed, out_w, 0, g)
    for g in range(groups):
        attn = gather_sum(sums[g], 0, g)
        first = (x_in[g, rank].astype(jnp.float32) + attn).astype(jnp.bfloat16)
        first_own[g] = first
        for k in order:
            first_copy(g, k).start()
        first_in[g, rank] = first
    for load in loads[5:]:
        load.wait()
    for g in range(groups):
        for k in order:
            p = other(k)
            arrival(first_in.at[g, p], first_recv.at[g, p]).wait_recv()
        sums[g] = scatter(feed(g), down_w, 1, g)
    for g in range(groups):
        lower = gather_sum(sums[g], 1, g)
        result = (first_own[g].astype(jnp.float32) + lower).astype(jnp.bfloat16)
        next_own[g] = result

        @pl.when(segment < segments - 1)
        def _():
            for k in [*order, 0]:
                next_copy(g, k).start()

        out[g * rows : (g + 1) * rows] = result

    for g in range(groups):

        @pl.when(segment == 0)
        def _():
            for k in order:
                x_copy(g, k).wait_send()

        for k in order:
            part_copy(0, g, k).wait_send()
            first_copy(g, k).wait_send()
            part_copy(1, g, k).wait_send()

        @pl.when(segment < segments - 1)
        def _():
            for k in [*order, 0]:
                next_copy(g, k).wait_send()


def body(
    embeds,
    norm_gains,
    w_qkv,
    w_out,
    w_up,
    w_down,
    cache,
    lengths,
    active_heads,
    active_blocks,
    active_counts,
):
    segments = lax.axis_size("segment")
    members = lax.axis_size("tensor")
    steps, seqs, piece = embeds.shape
    micro = active_heads.shape[2]
    width = piece * members
    head_dim = w_qkv.shape[-1]
    block = w_up.shape[2]
    positions = cache.shape[4]
    groups = GROUPS
    rows = steps * seqs // groups
    bf16 = jnp.bfloat16
    vmem = pl.BlockSpec(memory_space=pltpu.VMEM)
    smem = pl.BlockSpec(memory_space=pltpu.SMEM)
    hbm = pl.BlockSpec(memory_space=pl.ANY)
    dma = pltpu.SemaphoreType.DMA
    sizes = (segments, members, steps, seqs, micro, groups)
    flops = 2 * steps * seqs * width * (4 * head_dim + 2 * block)
    states = pl.pallas_call(
        functools.partial(relay_kernel, sizes),
        out_shape=jax.ShapeDtypeStruct((steps * seqs, piece), bf16),
        in_specs=[vmem, vmem, hbm, hbm, hbm, hbm, hbm, smem, smem, smem, smem],
        out_specs=vmem,
        scratch_shapes=[
            pltpu.VMEM((width, 3 * head_dim), bf16),
            pltpu.VMEM((head_dim, width), bf16),
            pltpu.VMEM((width, block), bf16),
            pltpu.VMEM((block, width), bf16),
            pltpu.VMEM((2, seqs * positions, head_dim), bf16),
            dma((7,)),
            pltpu.VMEM((groups, members, rows, piece), bf16),
            pltpu.VMEM((groups, members, rows, piece), bf16),
            pltpu.VMEM((2, groups, members, rows, piece), bf16),
            pltpu.VMEM((2, groups, members, rows, piece), bf16),
            dma((groups, members)),
            dma((groups, members)),
            dma((2, groups, members)),
            dma((groups, members)),
            dma((groups, members)),
            dma((2, groups, members)),
            dma((groups, members)),
            pltpu.VMEM((groups, rows, piece), bf16),
            pltpu.VMEM((groups, rows, piece), bf16),
        ],
        compiler_params=pltpu.CompilerParams(
            collective_id=0, has_side_effects=True, vmem_limit_bytes=48 * 1024 * 1024
        ),
        cost_estimate=pl.CostEstimate(
            flops=flops, bytes_accessed=2 * width * (4 * head_dim + 2 * block), transcendentals=0
        ),
    )(
        embeds.reshape(steps * seqs, piece),
        norm_gains[0],
        jnp.transpose(w_qkv, (0, 2, 3, 1, 4)).reshape(3, width, head_dim),
        w_out[0, 0],
        w_up[0],
        w_down[0],
        cache.reshape(2, seqs * positions, head_dim),
        lengths,
        active_heads[0],
        active_blocks[0],
        active_counts[0],
    )
    return states.reshape(1, steps, seqs, piece)


def solution(mesh):
    in_specs = (
        P(None, None, "tensor"),
        P("segment", None, None),
        P("segment", None, None, "tensor", None),
        P("segment", "tensor", None, None),
        P("segment", None, "tensor"),
        P("segment", "tensor", None),
        P("segment", None, None, "tensor", None, None),
        P(),
        P("segment", None, None, None),
        P("segment", None, None, None),
        P("segment", None, None, None),
    )
    out_specs = P("segment", None, None, "tensor")
    return jax.shard_map(body, mesh=mesh, in_specs=in_specs, out_specs=out_specs, check_vma=False)
```

time: 1210 us -> 137 us (0.11)
  waiting for transfers between devices: 969 us -> 0 us
  Pallas kernels: 0 us -> 126 us
  other arithmetic: 63.4 us -> 0 us
  matrix products: 53.1 us -> 0 us
  local copies, waits for them, and re-layouts: 61 us -> 10.2 us
  blocking collectives: 27 us -> 0 us
  between operations: 13.1 us -> 0.02 us
    psum x14 -> x0, waiting for transfers between devices: 950 us -> none  [the longest x7 478 us: layer(): lax.psum(lower, 'tensor')]
    pallas_call x0 -> x1, Pallas kernels: none -> 126 us  [body(): pl.pallas_call(functools.partial(relay_kernel, sizes), out_shape=jax.Shap...]
    dot_general x48 -> x0, matrix products: 53.1 us -> none  [the longest x7 21.8 us: attend(): jnp.dot(h, projection, preferred_element_type=jnp.float32)]
    dynamic_slice x28 -> x0, local copies, waits for them, and re-layouts: 32.3 us -> none  [the longest x7 9.18 us: tick(): lax.dynamic_slice(states, (step, batch * group, 0), (1, group, piece))[0]]
    all_gather x1 -> x0, blocking collectives: 27 us -> none  [body(): source = lax.all_gather(embeds, 'tensor', axis=2, tiled=True)]
    reduce_sum x35 -> x0, other arithmetic: 19.6 us -> none  [the longest x14 15 us: normalize_whole(): mean = jnp.mean(values, -1, keepdims=True)]
    ppermute x7 -> x0, waiting for transfers between devices: 18.5 us -> none  [shifted(): return lax.ppermute(array, axis, pairs)]
    select_n x14 -> x0, other arithmetic: 15.3 us -> none  [the longest x7 8.57 us: tick(): fresh = jnp.where(valid, fresh_new, fresh)]
  transfers between devices with their start and end apart: 21 -> 0, of which waited for: 21 -> 0; matrix products, arithmetic and copies ran while one was open for 3% -> 0% of each run, Pallas kernels for 0% -> 0%
where the time goes in v1:
time: 137 us; the launch traced here: 136 us
  Pallas kernels  126 us (92%)
  local copies, waits for them, and re-layouts  10.2 us (7%)
    pallas_call x1, Pallas kernels, body(): pl.pallas_call(functools.partial(relay_kernel, sizes), out_shape=jax.Shap...  126 us
    unnamed x21, local copies, waits for them, and re-layouts  10.2 us

profile of v1, /device:TPU:3, one launch (start us, length us, event | category | flops | bytes accessed | tf_op | source)
XLA Modules:
  0.0 136.2 jit_solution(1196483983171516475)
XLA Ops:
  0.0 0.0 copy-start
  0.0 1.4 %copy-done = bf16[1,1,128,6144]{3,2,1,0:T(8,128)(2,1)S(1)} copy-done((bf16[1,1,128,6144]{3,2,1,0:T(8,128)(2,1)S(1)}, bf16[1,1,128,6144]{3,2,1,0:T(8,128)(2,1)}, u32[]{:S(2)}) %copy-start) | copy-done | bytes 1572888
  1.4 0.0 copy-start.1
  1.4 1.4 %copy-done.1 = bf16[1,6144,128]{2,1,0:T(8,128)(2,1)S(1)} copy-done((bf16[1,6144,128]{2,1,0:T(8,128)(2,1)S(1)}, bf16[1,6144,128]{2,1,0:T(8,128)(2,1)}, u32[]{:S(2)}) %copy-start.1) | copy-done | bytes 1572888
  2.8 0.0 copy-start.2
  2.8 1.4 %copy-done.2 = bf16[1,128,6144]{2,1,0:T(8,128)(2,1)S(1)} copy-done((bf16[1,128,6144]{2,1,0:T(8,128)(2,1)S(1)}, bf16[1,128,6144]{2,1,0:T(8,128)(2,1)}, u32[]{:S(2)}) %copy-start.2) | copy-done | bytes 1572888
  4.2 0.0 copy-start.3
  4.2 1.0 copy-done.3
  5.3 0.0 copy-start.4
  5.3 0.8 copy-done.4
  6.1 0.0 copy-start.5
  6.1 0.8 copy-done.5
  6.9 0.0 copy-start.6
  6.9 0.7 copy-done.6
  7.5 0.0 copy-start.7
  7.5 0.7 copy-done.7
  8.2 0.0 copy-start.8
  8.2 0.7 copy-done.8
  8.9 0.0 copy-start.9
  8.9 0.7 copy-done.9
  9.6 126.0 %shard_map.109 = bf16[32,768]{1,0:T(8,128)(2,1)S(1)} custom-call(bf16[32,768]{1,0:T(8,128)(2,1)S(1)} %bitcast.20, f32[2,6144]{1,0:T(2,128)S(1)} %bitcast.21, bf16[3,6144,128]{2,1,0:T(8,128)(2,1)} %bitcast.25, bf16[128,6144]{1,0:T(8,128)(2,1)S(1)} %bitcast.15, bf16[6144,128]{1,0:T(8,128)(2,1)S(1)} %bitcast.16, bf16[128,6144]{1,0:T(8,128)(2,1)S(1)} %bitcast.17, ...), custom_call_target="tpu_custom_call" | custom-call | flops 301989888 | bytes 9437184 | tf_op jit(solution)/shard_map/pallas_call | solution.py:360
  135.5 0.6 copy.14
Async XLA Ops:
  0.0 1.4 %copy-start = (bf16[1,1,128,6144]{3,2,1,0:T(8,128)(2,1)S(1)}, bf16[1,1,128,6144]{3,2,1,0:T(8,128)(2,1)}, u32[]{:S(2)}) copy-start(bf16[1,1,128,6144]{3,2,1,0:T(8,128)(2,1)} %param.14) | copy-start | bytes 4718596
  1.4 1.4 %copy-start.1 = (bf16[1,6144,128]{2,1,0:T(8,128)(2,1)S(1)}, bf16[1,6144,128]{2,1,0:T(8,128)(2,1)}, u32[]{:S(2)}) copy-start(bf16[1,6144,128]{2,1,0:T(8,128)(2,1)} %param.15) | copy-start | bytes 4718596
  2.8 1.4 %copy-start.2 = (bf16[1,128,6144]{2,1,0:T(8,128)(2,1)S(1)}, bf16[1,128,6144]{2,1,0:T(8,128)(2,1)}, u32[]{:S(2)}) copy-start(bf16[1,128,6144]{2,1,0:T(8,128)(2,1)} %param.16) | copy-start | bytes 4718596
  4.2 1.0 copy-start.3
  5.3 0.8 copy-start.4
  6.1 0.8 copy-start.5
  6.9 0.7 copy-start.6
  7.5 0.7 copy-start.7
  8.2 0.7 copy-start.8
  8.9 0.7 copy-start.9

commit v2 on v1

--- a/solution.py
+++ b/solution.py
@@ -8,7 +8,7 @@
 from jax.sharding import PartitionSpec as P
 
 EPS = 1e-05
-GROUPS = 1
+GROUPS = 2
 MESH_ID = pl.DeviceIdType.MESH
 
 
@@ -18,18 +18,25 @@
 
 def relay_kernel(
     sizes,
-    embeds,
-    gains,
+    embeds_at,
+    gains_at,
     w_qkv,
     w_out,
     w_up,
     w_down,
     cache,
+    lengths_at,
+    heads_at,
+    blocks_at,
+    counts_at,
+    out,
+    embeds,
+    gains,
     lengths,
     heads,
     blocks,
     counts,
-    out,
+    small_sem,
     qkv_w,
     out_w,
     up_w,
@@ -65,6 +72,21 @@
     def other(k):
         return lax.rem(rank + k, members)
 
+    small = [
+        pltpu.make_async_copy(source, target, small_sem.at[i])
+        for i, (source, target) in enumerate(
+            [
+                (embeds_at, embeds),
+                (lengths_at, lengths),
+                (heads_at, heads),
+                (blocks_at, blocks),
+                (counts_at, counts),
+                (gains_at, gains),
+            ]
+        )
+    ]
+    for load in small:
+        load.start()
     loads = [
         pltpu.make_async_copy(
             w_qkv.at[j], qkv_w.at[:, pl.ds(j * head_dim, head_dim)], load_sem.at[j]
@@ -128,6 +150,8 @@
             (segment, other(k)),
         )
 
+    small[0].wait()
+
     @pl.when(segment == 0)
     def _():
         for g in range(groups):
@@ -135,6 +159,8 @@
                 x_copy(g, k).start()
             x_in[g, rank] = embeds[g * rows : (g + 1) * rows]
 
+    for load in small[1:]:
+        load.wait()
     row_ids = lax.broadcasted_iota(jnp.int32, (steps * seqs, 1), 0)
     row_seq = lax.rem(row_ids, seqs)
     row_len = jnp.zeros((steps * seqs, 1), jnp.int32)
@@ -352,7 +378,6 @@
     rows = steps * seqs // groups
     bf16 = jnp.bfloat16
     vmem = pl.BlockSpec(memory_space=pltpu.VMEM)
-    smem = pl.BlockSpec(memory_space=pltpu.SMEM)
     hbm = pl.BlockSpec(memory_space=pl.ANY)
     dma = pltpu.SemaphoreType.DMA
     sizes = (segments, members, steps, seqs, micro, groups)
@@ -360,9 +385,16 @@
     states = pl.pallas_call(
         functools.partial(relay_kernel, sizes),
         out_shape=jax.ShapeDtypeStruct((steps * seqs, piece), bf16),
-        in_specs=[vmem, vmem, hbm, hbm, hbm, hbm, hbm, smem, smem, smem, smem],
+        in_specs=[hbm] * 11,
         out_specs=vmem,
         scratch_shapes=[
+            pltpu.VMEM((steps * seqs, piece), bf16),
+            pltpu.VMEM(norm_gains.shape[1:], jnp.float32),
+            pltpu.SMEM(lengths.shape, jnp.int32),
+            pltpu.SMEM(active_heads.shape[1:], jnp.int32),
+            pltpu.SMEM(active_blocks.shape[1:], jnp.int32),
+            pltpu.SMEM(active_counts.shape[1:], jnp.int32),
+            dma((6,)),
             pltpu.VMEM((width, 3 * head_dim), bf16),
             pltpu.VMEM((head_dim, width), bf16),
             pltpu.VMEM((width, block), bf16),
@@ -384,7 +416,7 @@
             pltpu.VMEM((groups, rows, piece), bf16),
         ],
         compiler_params=pltpu.CompilerParams(
-            collective_id=0, has_side_effects=True, vmem_limit_bytes=48 * 1024 * 1024
+            collective_id=0, has_side_effects=True, vmem_limit_bytes=56 * 1024 * 1024
         ),
         cost_estimate=pl.CostEstimate(
             flops=flops, bytes_accessed=2 * width * (4 * head_dim + 2 * block), transcendentals=0

time: 137 us -> 106 us (0.77)
  Pallas kernels: 126 us -> 104 us
  local copies, waits for them, and re-layouts: 10.2 us -> 1.42 us
    pallas_call x1, Pallas kernels: 126 us -> 104 us  [body(): pl.pallas_call(functools.partial(relay_kernel, sizes), out_shape=jax.Shap...]
    unnamed x21 -> x1, local copies, waits for them, and re-layouts: 10.2 us -> 1.42 us
where the time goes in v2:
time: 106 us
  Pallas kernels  104 us (98%)
  local copies, waits for them, and re-layouts  1.42 us (1%)
    pallas_call x1, Pallas kernels, body(): pl.pallas_call(functools.partial(relay_kernel, sizes), out_shape=jax.Shap...  104 us

profile of v2, /device:TPU:3, one launch (start us, length us, event | category | flops | bytes accessed | tf_op | source)
XLA Modules:
  0.0 105.5 jit_solution(10927500177099342097)
XLA Ops:
  0.0 104.1 %shard_map.109 = bf16[32,768]{1,0:T(8,128)(2,1)} custom-call(bf16[32,768]{1,0:T(8,128)(2,1)} %bitcast.21, f32[2,6144]{1,0:T(2,128)} %bitcast.22, bf16[3,6144,128]{2,1,0:T(8,128)(2,1)} %bitcast.15, bf16[128,6144]{1,0:T(8,128)(2,1)} %bitcast.16, bf16[6144,128]{1,0:T(8,128)(2,1)} %bitcast.17, bf16[128,6144]{1,0:T(8,128)(2,1)} %bitcast.18, ...), custom_call_target="tpu_custom_call" | custom-call | flops 301989888 | bytes 9437184 | tf_op jit(solution)/shard_map/pallas_call | solution.py:385
  104.1 1.4 %copy.14 = bf16[1,2,16,768]{3,2,1,0:T(8,128)(2,1)} copy(bf16[1,2,16,768]{3,2,1,0:T(8,128)(2,1)} %bitcast.20) | data formatting | bytes 98304

commit v3 on v2

--- a/solution.py
+++ b/solution.py
@@ -13,7 +13,7 @@
 
 
 def partner_order(members):
-    return sorted(range(1, members), key=lambda k: (-min(k, members - k), k))
+    return list(range(1, members))
 
 
 def relay_kernel(
@@ -220,7 +220,7 @@
         return jnp.dot(values, weight[:, columns(rank)], preferred_element_type=jnp.float32)
 
     def gather_sum(total, phase, g):
-        for k in reversed(order):
+        for k in order:
             p = other(k)
             arrival(part_in.at[phase, g, p], part_recv.at[phase, g, p]).wait_recv()
             total = total + part_in[phase, g, p].astype(jnp.float32)

time: 106 us -> 99.3 us (0.937)
  Pallas kernels: 104 us -> 97.5 us
    pallas_call x1, Pallas kernels: 104 us -> 97.5 us  [body(): pl.pallas_call(functools.partial(relay_kernel, sizes), out_shape=jax.Shap...]
where the time goes in v3:
time: 99.3 us; the launch traced here: 98.9 us
  Pallas kernels  97.5 us (98%)
  local copies, waits for them, and re-layouts  1.42 us (1%)
    pallas_call x1, Pallas kernels, body(): pl.pallas_call(functools.partial(relay_kernel, sizes), out_shape=jax.Shap...  97.5 us

profile of v3, /device:TPU:3, one launch (start us, length us, event | category | flops | bytes accessed | tf_op | source)
XLA Modules:
  0.0 98.9 jit_solution(1453390261361961674)
XLA Ops:
  0.0 97.5 %shard_map.109 = bf16[32,768]{1,0:T(8,128)(2,1)} custom-call(bf16[32,768]{1,0:T(8,128)(2,1)} %bitcast.21, f32[2,6144]{1,0:T(2,128)} %bitcast.22, bf16[3,6144,128]{2,1,0:T(8,128)(2,1)} %bitcast.15, bf16[128,6144]{1,0:T(8,128)(2,1)} %bitcast.16, bf16[6144,128]{1,0:T(8,128)(2,1)} %bitcast.17, bf16[128,6144]{1,0:T(8,128)(2,1)} %bitcast.18, ...), custom_call_target="tpu_custom_call" | custom-call | flops 301989888 | bytes 9437184 | tf_op jit(solution)/shard_map/pallas_call | solution.py:385
  97.5 1.4 %copy.14 = bf16[1,2,16,768]{3,2,1,0:T(8,128)(2,1)} copy(bf16[1,2,16,768]{3,2,1,0:T(8,128)(2,1)} %bitcast.20) | data formatting | bytes 98304

commit v4 on v3

--- a/solution.py
+++ b/solution.py
@@ -213,17 +213,23 @@
         )
 
     def scatter(values, weight, phase, g):
-        for k in order:
-            part = jnp.dot(values, weight[:, columns(other(k))], preferred_element_type=jnp.float32)
-            part_out[phase, g, k] = part.astype(jnp.bfloat16)
-            part_copy(phase, g, k).start()
+        for first in range(0, len(order), (members // 2)):
+            batch = order[first : first + (members // 2)]
+            for k in batch:
+                part = jnp.dot(
+                    values, weight[:, columns(other(k))], preferred_element_type=jnp.float32
+                )
+                part_out[phase, g, k] = part.astype(jnp.bfloat16)
+            for k in batch:
+                part_copy(phase, g, k).start()
         return jnp.dot(values, weight[:, columns(rank)], preferred_element_type=jnp.float32)
 
     def gather_sum(total, phase, g):
         for k in order:
             p = other(k)
             arrival(part_in.at[phase, g, p], part_recv.at[phase, g, p]).wait_recv()
-            total = total + part_in[phase, g, p].astype(jnp.float32)
+        for k in order:
+            total = total + part_in[phase, g, other(k)].astype(jnp.float32)
         return total
 
     def first_copy(g, k):

time: 99.3 us -> 96.7 us (0.974)
  Pallas kernels: 97.5 us -> 95.1 us
    pallas_call x1, Pallas kernels: 97.5 us -> 95.1 us  [body(): pl.pallas_call(functools.partial(relay_kernel, sizes), out_shape=jax.Shap...]
where the time goes in v4:
time: 96.7 us; the launch traced here: 96.6 us
  Pallas kernels  95.1 us (98%)
  local copies, waits for them, and re-layouts  1.42 us (1%)
    pallas_call x1, Pallas kernels, body(): pl.pallas_call(functools.partial(relay_kernel, sizes), out_shape=jax.Shap...  95.1 us

profile of v4, /device:TPU:3, one launch (start us, length us, event | category | flops | bytes accessed | tf_op | source)
XLA Modules:
  0.0 96.6 jit_solution(4771127691068662926)
XLA Ops:
  0.0 95.1 %shard_map.109 = bf16[32,768]{1,0:T(8,128)(2,1)} custom-call(bf16[32,768]{1,0:T(8,128)(2,1)} %bitcast.21, f32[2,6144]{1,0:T(2,128)} %bitcast.22, bf16[3,6144,128]{2,1,0:T(8,128)(2,1)} %bitcast.15, bf16[128,6144]{1,0:T(8,128)(2,1)} %bitcast.16, bf16[6144,128]{1,0:T(8,128)(2,1)} %bitcast.17, bf16[128,6144]{1,0:T(8,128)(2,1)} %bitcast.18, ...), custom_call_target="tpu_custom_call" | custom-call | flops 301989888 | bytes 9437184 | tf_op jit(solution)/shard_map/pallas_call | solution.py:391
  95.1 1.4 %copy.14 = bf16[1,2,16,768]{3,2,1,0:T(8,128)(2,1)} copy(bf16[1,2,16,768]{3,2,1,0:T(8,128)(2,1)} %bitcast.20) | data formatting | bytes 98304
